TPU v7x, 256 devices: a whole 4x4x8 slice. The times are simulated.
256 devices in a mesh: dp: 16 (over x_lo, y, core), tensor: 16 (over z, x_hi).
Axes of the slice: x: 4 (x_hi: 2, x_lo: 2; x = x_hi * 2 + x_lo), y: 4, z: 8, core: 2. Of those that a mesh axis runs over, the one named last changes fastest.
Arguments:
- tokens: bfloat16 [2048, 32768], P('dp', 'tensor'), may hold values from -6 to 6
- factors: bfloat16 [8, 256, 2, 128, 128], P(None, 'tensor'), may hold values from -0.375 to 0.375
- cotangent: bfloat16 [2048, 32768], P('dp', 'tensor'), may hold values from -6 to 6
Outputs:
- mixed: bfloat16 [2048, 32768], P('dp', 'tensor')
- token_grad: bfloat16 [2048, 32768], P('dp', 'tensor')
- factor_grad: float32 [8, 256, 2, 128, 128], P(None, 'tensor', None, 'dp')
All inputs are finite; a program needn't handle non-finite values.
Results may differ from a plain program's by a relative error of at most 0.017.
Values may be sent and summed in bfloat16 or wider, within the bound.
A program may use at most 128 MiB of HBM per device.

v0:
```python
import jax
import jax.numpy as jnp
from jax import lax
from jax.sharding import PartitionSpec as P


def partner_2(block, axis, stride):
    count = lax.axis_size(axis)
    route = []
    for low in range(count):
        high = low | 1 << stride
        if high != low and high < count:
            route += [(low, high), (high, low)]
    return lax.ppermute(block, axis, route)


def pair_flip(x, dist):
    t, b, f = x.shape
    r = x.reshape(t, b // (2 * dist), 2, dist, f)
    return jnp.flip(r, 2).reshape(t, b, f)


def mix_level(x, partner, weight):
    stacked = jnp.stack([x, partner], 2)
    return jnp.einsum("tbki,bkio->tbo", stacked, weight, preferred_element_type=jnp.float32).astype(
        jnp.bfloat16
    )


def back_terms(grad, weight):
    own = jnp.einsum("tbo,bio->tbi", grad, weight[:, 0], preferred_element_type=jnp.float32)
    cross = jnp.einsum(
        "tbo,bio->tbi", grad, weight[:, 1], preferred_element_type=jnp.float32
    ).astype(jnp.bfloat16)
    return (own, cross)


def weight_grad(x, partner, grad):
    stacked = jnp.stack([x, partner], 2)
    return jnp.einsum("tbki,tbo->bkio", stacked, grad, preferred_element_type=jnp.float32)


def reduce_all(dw_stack):
    return lax.psum_scatter(dw_stack, "dp", scatter_dimension=3, tiled=True)


def per_device(tokens, factors, cotangent):
    rows = tokens.shape[0]
    nblocks = factors.shape[1]
    width = factors.shape[3]
    levels = factors.shape[0]
    local_bits = nblocks.bit_length() - 1
    x = tokens.reshape(rows, nblocks, width)
    grad_in = cotangent.reshape(rows, nblocks, width)
    saved = []
    for level in range(local_bits):
        partner = pair_flip(x, 2**level)
        saved.append((x, partner))
        x = mix_level(x, partner, factors[level])
    grads = [None] * levels
    for level in range(local_bits, levels):
        partner = partner_2(x, "tensor", level - local_bits)
        saved.append((x, partner))
        x = mix_level(x, partner, factors[level])
    grad = grad_in
    for level in reversed(range(levels)):
        own, cross = back_terms(grad, factors[level])
        if level < local_bits:
            moved = pair_flip(cross, 2**level)
        else:
            moved = partner_2(cross, "tensor", level - local_bits)
        moved = lax.optimization_barrier(moved)
        grads[level] = weight_grad(saved[level][0], saved[level][1], grad)
        grad = (own + moved.astype(jnp.float32)).astype(jnp.bfloat16)
    factor_grad = reduce_all(jnp.stack(grads, 0))
    return (x.reshape(rows, nblocks * width), grad.reshape(rows, nblocks * width), factor_grad)


def solution(mesh):
    placed = (P("dp", "tensor"), P(None, "tensor", None, None, None), P("dp", "tensor"))
    return jax.shard_map(
        per_device,
        mesh=mesh,
        in_specs=placed,
        out_specs=(P("dp", "tensor"), P("dp", "tensor"), P(None, "tensor", None, "dp", None)),
        check_vma=False,
    )
```

profile of v0, /device:TPU:1, one launch (start us, length us, event | category | flops | bytes accessed | tf_op | source)
XLA Modules:
  0.0 277.8 jit_solution(7389774287769404148)
XLA Ops:
  7.2 5.8 %slice_bitcast_fusion.6 = (bf16[16,2,128,128]{3,2,1,0:T(8,128)(2,1)}, bf16[16,2,128,128]{3,2,1,0:T(8,128)(2,1)}, bf16[16,2,128,128]{3,2,1,0:T(8,128)(2,1)}, bf16...) fusion(bf16[8,16,2,128,128]{4,3,2,1,0:T(8,128)(2,1)} %param.4), kind=kLoop, calls=%fused_computation.87 | loop fusion | bytes 17825792 | tf_op jit(solution)/shard_map/squeeze | solution.py:59
  13.0 3.0 %copy.110 = bf16[1,16,2,128,128]{3,4,2,1,0:T(8,128)(2,1)} copy(bf16[1,16,2,128,128]{4,3,2,1,0:T(8,128)(2,1)} %get-tuple-element.16) | data formatting | bytes 2097152
  16.0 2.4 fusion.22
  18.4 7.7 %collective-permute-start.4 = (bf16[128,16,128]{0,2,1:T(8,128)(2,1)}, bf16[128,16,128]{0,2,1:T(8,128)(2,1)}, u32[]{:S(2)}, u32[]{:S(2)}) collective-permute-start(bf16[128,16,128]{0,2,1:T(8,128)(2,1)} %fusion.22), channel_id=1, source_target_pairs={{0,8},{8,0},{1,9},{9,1},{2,10},{10,2},{3,11},{11,3},{4,12},{12,4},... | collective-permute-start | bytes 1572872 | tf_op jit(solution)/shard_map/ppermute | solution.py:14
  28.3 2.0 copy.35
  31.4 2.2 copy.36
  33.6 2.6 fusion.7
  43.3 2.0 fusion.10
  45.3 2.8 %collective-permute-start = (bf16[128,16,128]{2,0,1:T(8,128)(2,1)S(1)}, bf16[128,16,128]{2,0,1:T(8,128)(2,1)S(1)}, u32[]{:S(2)}, u32[]{:S(2)}) collective-permute-start(bf16[128,16,128]{2,0,1:T(8,128)(2,1)S(1)} %bitcast.319), channel_id=1, source_target_pairs={{0,1},{1,0},{2,3},{3,2},{4,5},{5,4},{6,7},{7,6},{8,9},{9,8},{10,11... | collective-permute-start | bytes 1572872 | tf_op jit(solution)/shard_map/ppermute | solution.py:14
  53.7 5.6 %collective-permute-done = bf16[128,16,128]{2,0,1:T(8,128)(2,1)S(1)} collective-permute-done((bf16[128,16,128]{2,0,1:T(8,128)(2,1)S(1)}, bf16[128,16,128]{2,0,1:T(8,128)(2,1)S(1)}, u32[]{:S(2)}, u32[]{:S(2)}) %collective-permute-start) | collective-permute-done | bytes 524320 | tf_op jit(solution)/shard_map/ppermute | solution.py:14
  62.1 16.0 %collective-permute-done.5 = bf16[128,16,128]{2,0,1:T(8,128)(2,1)S(1)} collective-permute-done((bf16[128,16,128]{2,0,1:T(8,128)(2,1)S(1)}, bf16[128,16,128]{2,0,1:T(8,128)(2,1)S(1)}, u32[]{:S(2)}, u32[]{:S(2)}) %collective-permute-start.5) | collective-permute-done | bytes 524320 | tf_op jit(solution)/shard_map/ppermute | solution.py:14
  81.2 2.4 collective-permute-done.1
  85.6 15.8 %collective-permute-done.6 = bf16[128,16,128]{2,0,1:T(8,128)(2,1)S(1)} collective-permute-done((bf16[128,16,128]{2,0,1:T(8,128)(2,1)S(1)}, bf16[128,16,128]{2,0,1:T(8,128)(2,1)S(1)}, u32[]{:S(2)}, u32[]{:S(2)}) %collective-permute-start.6) | collective-permute-done | bytes 524320 | tf_op jit(solution)/shard_map/ppermute | solution.py:14
  104.7 4.6 %collective-permute-start.3 = (bf16[128,16,128]{2,0,1:T(8,128)(2,1)}, bf16[128,16,128]{2,0,1:T(8,128)(2,1)}, u32[]{:S(2)}, u32[]{:S(2)}) collective-permute-start(bf16[128,16,128]{2,0,1:T(8,128)(2,1)} %bitcast.38), channel_id=1, source_target_pairs={{0,8},{8,0},{1,9},{9,1},{2,10},{10,2},{3,11},{11,3},{4,12},{12,4},... | collective-permute-start | bytes 1572872 | tf_op jit(solution)/shard_map/ppermute | solution.py:14
  109.3 5.7 %collective-permute-done.7 = bf16[128,16,128]{2,0,1:T(8,128)(2,1)S(1)} collective-permute-done((bf16[128,16,128]{2,0,1:T(8,128)(2,1)S(1)}, bf16[128,16,128]{2,0,1:T(8,128)(2,1)S(1)}, u32[]{:S(2)}, u32[]{:S(2)}) %collective-permute-start.7) | collective-permute-done | bytes 524320 | tf_op jit(solution)/shard_map/ppermute | solution.py:14
  122.7 2.5 convolution_convert_fusion.1
  127.1 2.0 fusion.20
  129.1 3.0 %bitcast_dynamic-update-slice_fusion.7 = f32[8,16,2,128,128]{4,3,2,1,0:T(8,128)} fusion(bf16[128,16,1,128]{3,0,2,1:T(8,128)(2,1)} %bitcast.302, bf16[128,16,1,128]{3,0,2,1:T(8,128)(2,1)} %copy.36, bf16[128,16,128]{2,0,1:T(8,128)(2,1)S(1)} %fusion.20), kind=kOutput, calls=%fused_computation.7 | convolution fusion | flops 134742016 | bytes 3670016 | tf_op jit(solution)/shard_map/tbki,tbo->bkio/dot_general | solution.py:40
  132.2 3.2 %bitcast_dynamic-update-slice_fusion.6 = f32[8,16,2,128,128]{4,3,2,1,0:T(8,128)} fusion(f32[8,16,2,128,128]{4,3,2,1,0:T(8,128)} %bitcast_dynamic-update-slice_fusion.7, bf16[128,16,128]{2,0,1:T(8,128)(2,1)} %copy-done, bf16[128,16,1,128]{3,0,1,2:T(8,128)(2,1)} %bitcast.307, bf16[128,16,1,128]{3,0,1,2:T(8,128)(2,1)} %bitcast.305), kind=kOutput, calls=%fused_computation.6 | convolution fusion | flops 134742016 | bytes 3670016 | tf_op jit(solution)/shard_map/tbki,tbo->bkio/dot_general | solution.py:40
  135.3 3.1 %bitcast_dynamic-update-slice_fusion.5 = f32[8,16,2,128,128]{4,3,2,1,0:T(8,128)} fusion(f32[8,16,2,128,128]{4,3,2,1,0:T(8,128)} %bitcast_dynamic-update-slice_fusion.6, bf16[128,16,128]{2,0,1:T(8,128)(2,1)S(1)} %fusion.18, bf16[128,16,1,128]{3,0,1,2:T(8,128)(2,1)} %bitcast.300, bf16[128,16,1,128]{3,0,1,2:T(8,128)(2,1)} %bitcast.298), kind=kOutput, calls=%fused_computation.5 | convolution fusion | flops 134742016 | bytes 3670016 | tf_op jit(solution)/shard_map/tbki,tbo->bkio/dot_general | solution.py:40
  138.4 3.1 %bitcast_dynamic-update-slice_fusion.4 = f32[8,16,2,128,128]{4,3,2,1,0:T(8,128)} fusion(f32[8,16,2,128,128]{4,3,2,1,0:T(8,128)} %bitcast_dynamic-update-slice_fusion.5, bf16[128,16,128]{2,0,1:T(8,128)(2,1)S(1)} %fusion.17, bf16[128,16,1,128]{3,0,1,2:T(8,128)(2,1)} %bitcast.295, bf16[128,16,1,128]{3,0,1,2:T(8,128)(2,1)} %bitcast.293), kind=kOutput, calls=%fused_computation.4 | convolution fusion | flops 134742016 | bytes 3670016 | tf_op jit(solution)/shard_map/tbki,tbo->bkio/dot_general | solution.py:40
  147.0 3.0 %bitcast_dynamic-update-slice_fusion = f32[8,16,2,128,128]{4,3,2,1,0:T(8,128)} fusion(f32[8,16,2,128,128]{4,3,2,1,0:T(8,128)} %bitcast_dynamic-update-slice_fusion.1, bf16[128,16,128,1]{2,1,0,3:T(8,128)(2,1)S(1)} %bitcast.308, bf16[128,16,1,128]{3,0,1,2:T(8,128)(2,1)} %bitcast.40, bf16[128,16,1,128]{3,0,1,2:T(8,128)(2,1)} %bitcast.39), kind=kOutput, calls=%fused_computation | convolution fusion | flops 134742016 | bytes 3670016 | tf_op jit(solution)/shard_map/tbki,tbo->bkio/dot_general | solution.py:40
  150.0 2.0 fusion.14
  155.3 115.6 %reduce-scatter.2.cloned.1.call-done = f32[8,16,2,8,128]{4,3,2,1,0:T(8,128)} async-done(((f32[8,16,2,128,128]{4,3,2,1,0:T(8,128)}), f32[8,16,2,8,128]{4,3,2,1,0:T(8,128)}) %reduce-scatter.2.cloned.1.call-update) | async-done | bytes 1048592 | tf_op jit(solution)/shard_map/reduce_scatter | solution.py:44
  (98 shorter events, 45.3 us)
Async XLA Ops:
  7.2 19.0 %copy-start.13 = (bf16[128,2048]{1,0:T(8,128)(2,1)S(1)}, bf16[128,2048]{1,0:T(8,128)(2,1)}, u32[]{:S(2)}) copy-start(bf16[128,2048]{1,0:T(8,128)(2,1)} %param.3) | copy-start | bytes 1572868
  7.2 263.8 %reduce-scatter.2.cloned.1.call-start = ((), (), s32[]{:S(2)}) async-start(), calls=%async_computation.1 | async-start | bytes 17825792 | tf_op jit(solution)/shard_map/reduce_scatter | solution.py:44
  13.0 36.7 %copy-start.3 = (bf16[16,2,128,128]{3,2,1,0:T(8,128)(2,1)}, bf16[16,2,128,128]{3,2,1,0:T(8,128)(2,1)S(1)}, u32[]{:S(2)}) copy-start(bf16[16,2,128,128]{3,2,1,0:T(8,128)(2,1)S(1)} %get-tuple-element.15) | copy-start | bytes 3145732
  13.0 48.2 %copy-start.4 = (bf16[16,2,128,128]{3,2,1,0:T(8,128)(2,1)}, bf16[16,2,128,128]{3,2,1,0:T(8,128)(2,1)S(1)}, u32[]{:S(2)}) copy-start(bf16[16,2,128,128]{3,2,1,0:T(8,128)(2,1)S(1)} %get-tuple-element.14) | copy-start | bytes 3145732
  18.4 31.3 %collective-permute-start.4 = (bf16[128,16,128]{0,2,1:T(8,128)(2,1)}, bf16[128,16,128]{0,2,1:T(8,128)(2,1)}, u32[]{:S(2)}, u32[]{:S(2)}) collective-permute-start(bf16[128,16,128]{0,2,1:T(8,128)(2,1)} %fusion.22), channel_id=1, source_target_pairs={{0,8},{8,0},{1,9},{9,1},{2,10},{10,2},{3,11},{11,3},{4,12},{12,4},... | collective-permute-start | bytes 1572872 | tf_op jit(solution)/shard_map/ppermute | solution.py:14
  42.4 74.5 %copy-start.9 = (bf16[16,128,128]{2,1,0:T(8,128)(2,1)}, bf16[16,128,128]{2,1,0:T(8,128)(2,1)S(1)}, u32[]{:S(2)}) copy-start(bf16[16,128,128]{2,1,0:T(8,128)(2,1)S(1)} %fusion.9) | copy-start | bytes 1572868
  43.3 58.1 %copy-start.8 = (bf16[16,2,128,128]{3,2,1,0:T(8,128)(2,1)S(1)}, bf16[16,2,128,128]{3,2,1,0:T(8,128)(2,1)}, u32[]{:S(2)}) copy-start(bf16[16,2,128,128]{3,2,1,0:T(8,128)(2,1)} %get-tuple-element.11) | copy-start | bytes 3145732
  43.3 58.6 %copy-start.6 = (bf16[16,2,128,128]{3,2,1,0:T(8,128)(2,1)S(1)}, bf16[16,2,128,128]{3,2,1,0:T(8,128)(2,1)}, u32[]{:S(2)}) copy-start(bf16[16,2,128,128]{3,2,1,0:T(8,128)(2,1)} %get-tuple-element.12) | copy-start | bytes 3145732
  43.3 60.1 %copy-start.7 = (bf16[16,2,128,128]{3,2,1,0:T(8,128)(2,1)S(1)}, bf16[16,2,128,128]{3,2,1,0:T(8,128)(2,1)}, u32[]{:S(2)}) copy-start(bf16[16,2,128,128]{3,2,1,0:T(8,128)(2,1)} %get-tuple-element.17) | copy-start | bytes 3145732
  43.3 72.2 %copy-start.5 = (bf16[16,2,128,128]{3,2,1,0:T(8,128)(2,1)S(1)}, bf16[16,2,128,128]{3,2,1,0:T(8,128)(2,1)}, u32[]{:S(2)}) copy-start(bf16[16,2,128,128]{3,2,1,0:T(8,128)(2,1)} %get-tuple-element.13) | copy-start | bytes 3145732
  45.3 70.8 %copy-start.14 = (bf16[16,128,128]{2,1,0:T(8,128)(2,1)}, bf16[16,128,128]{2,1,0:T(8,128)(2,1)S(1)}, u32[]{:S(2)}) copy-start(bf16[16,128,128]{2,1,0:T(8,128)(2,1)S(1)} %fusion.10) | copy-start | bytes 1572868
  45.3 14.1 %collective-permute-start = (bf16[128,16,128]{2,0,1:T(8,128)(2,1)S(1)}, bf16[128,16,128]{2,0,1:T(8,128)(2,1)S(1)}, u32[]{:S(2)}, u32[]{:S(2)}) collective-permute-start(bf16[128,16,128]{2,0,1:T(8,128)(2,1)S(1)} %bitcast.319), channel_id=1, source_target_pairs={{0,1},{1,0},{2,3},{3,2},{4,5},{5,4},{6,7},{7,6},{8,9},{9,8},{10,11... | collective-permute-start | bytes 1572872 | tf_op jit(solution)/shard_map/ppermute | solution.py:14
  52.4 25.6 %collective-permute-start.5 = (bf16[128,16,128]{2,0,1:T(8,128)(2,1)S(1)}, bf16[128,16,128]{2,0,1:T(8,128)(2,1)S(1)}, u32[]{:S(2)}, u32[]{:S(2)}) collective-permute-start(bf16[128,16,128]{2,0,1:T(8,128)(2,1)S(1)} %fusion.23), channel_id=1, source_target_pairs={{0,4},{4,0},{1,5},{5,1},{2,6},{6,2},{3,7},{7,3},{8,12},{12,8},{9,1... | collective-permute-start | bytes 1572872 | tf_op jit(solution)/shard_map/ppermute | solution.py:14
  59.4 56.7 %copy-start.16 = (bf16[128,16,128]{2,0,1:T(8,128)(2,1)}, bf16[128,16,128]{2,0,1:T(8,128)(2,1)S(1)}, u32[]{:S(2)}) copy-start(bf16[128,16,128]{2,0,1:T(8,128)(2,1)S(1)} %collective-permute-done) | copy-start | bytes 1572868
  61.2 54.8 %copy-start.18 = (bf16[16,128,128]{2,1,0:T(8,128)(2,1)}, bf16[16,128,128]{2,1,0:T(8,128)(2,1)S(1)}, u32[]{:S(2)}) copy-start(bf16[16,128,128]{2,1,0:T(8,128)(2,1)S(1)} %fusion.11) | copy-start | bytes 1572868
  61.2 22.4 %collective-permute-start.1 = (bf16[128,16,128]{2,0,1:T(8,128)(2,1)S(1)}, bf16[128,16,128]{2,0,1:T(8,128)(2,1)S(1)}, u32[]{:S(2)}, u32[]{:S(2)}) collective-permute-start(bf16[128,16,128]{2,0,1:T(8,128)(2,1)S(1)} %bitcast.324), channel_id=1, source_target_pairs={{0,2},{2,0},{1,3},{3,1},{4,6},{6,4},{5,7},{7,5},{8,10},{10,8},{9,1... | collective-permute-start | bytes 1572872 | tf_op jit(solution)/shard_map/ppermute | solution.py:14
  81.1 20.3 %collective-permute-start.6 = (bf16[128,16,128]{2,0,1:T(8,128)(2,1)S(1)}, bf16[128,16,128]{2,0,1:T(8,128)(2,1)S(1)}, u32[]{:S(2)}, u32[]{:S(2)}) collective-permute-start(bf16[128,16,128]{2,0,1:T(8,128)(2,1)S(1)} %fusion.24), channel_id=1, source_target_pairs={{0,2},{2,0},{1,3},{3,1},{4,6},{6,4},{5,7},{7,5},{8,10},{10,8},{9,1... | collective-permute-start | bytes 1572872 | tf_op jit(solution)/shard_map/ppermute | solution.py:14
  85.5 23.8 %copy-start.22 = (bf16[16,128,128]{2,1,0:T(8,128)(2,1)}, bf16[16,128,128]{2,1,0:T(8,128)(2,1)S(1)}, u32[]{:S(2)}) copy-start(bf16[16,128,128]{2,1,0:T(8,128)(2,1)S(1)} %fusion.12) | copy-start | bytes 1572868
  85.5 17.9 %collective-permute-start.2 = (bf16[128,16,128]{2,0,1:T(8,128)(2,1)S(1)}, bf16[128,16,128]{2,0,1:T(8,128)(2,1)S(1)}, u32[]{:S(2)}, u32[]{:S(2)}) collective-permute-start(bf16[128,16,128]{2,0,1:T(8,128)(2,1)S(1)} %bitcast.329), channel_id=1, source_target_pairs={{0,4},{4,0},{1,5},{5,1},{2,6},{6,2},{3,7},{7,3},{8,12},{12,8},{9,1... | collective-permute-start | bytes 1572872 | tf_op jit(solution)/shard_map/ppermute | solution.py:14
  102.4 12.6 %collective-permute-start.7 = (bf16[128,16,128]{2,0,1:T(8,128)(2,1)S(1)}, bf16[128,16,128]{2,0,1:T(8,128)(2,1)S(1)}, u32[]{:S(2)}, u32[]{:S(2)}) collective-permute-start(bf16[128,16,128]{2,0,1:T(8,128)(2,1)S(1)} %fusion.25), channel_id=1, source_target_pairs={{0,1},{1,0},{2,3},{3,2},{4,5},{5,4},{6,7},{7,6},{8,9},{9,8},{10,11... | collective-permute-start | bytes 1572872 | tf_op jit(solution)/shard_map/ppermute | solution.py:14
  104.7 42.3 %collective-permute-start.3 = (bf16[128,16,128]{2,0,1:T(8,128)(2,1)}, bf16[128,16,128]{2,0,1:T(8,128)(2,1)}, u32[]{:S(2)}, u32[]{:S(2)}) collective-permute-start(bf16[128,16,128]{2,0,1:T(8,128)(2,1)} %bitcast.38), channel_id=1, source_target_pairs={{0,8},{8,0},{1,9},{9,1},{2,10},{10,2},{3,11},{11,3},{4,12},{12,4},... | collective-permute-start | bytes 1572872 | tf_op jit(solution)/shard_map/ppermute | solution.py:14
  127.1 18.1 %copy-start.23 = (bf16[16,128,128]{2,1,0:T(8,128)(2,1)S(1)}, bf16[16,128,128]{2,1,0:T(8,128)(2,1)}, u32[]{:S(2)}) copy-start(bf16[16,128,128]{2,1,0:T(8,128)(2,1)} %copy-done.22) | copy-start | bytes 1572868
  127.1 18.1 %copy-start.25 = (bf16[128,16,128]{2,0,1:T(8,128)(2,1)S(1)}, bf16[128,16,128]{2,0,1:T(8,128)(2,1)}, u32[]{:S(2)}) copy-start(bf16[128,16,128]{2,0,1:T(8,128)(2,1)} %copy-done.24) | copy-start | bytes 1572868
  127.1 19.8 %copy-start.12 = (bf16[16,8,16,128]{3,2,1,0:T(8,128)(2,1)S(1)}, bf16[16,8,16,128]{3,2,1,0:T(8,128)(2,1)}, u32[]{:S(2)}) copy-start(bf16[16,8,16,128]{3,2,1,0:T(8,128)(2,1)} %copy.113) | copy-start | bytes 1572868
  (11 other events, 106.5 us)
Sparse Core Ops, SparseCore 0:
  150.1 120.8 reduce-scatter.1
where the time goes:
time: 279 us; the launch traced here: 278 us
  waiting for transfers between devices  161 us (58%)
  matrix products  56.5 us (20%)
  local copies, waits for them, and re-layouts  26.9 us (10%)
  starting transfers between devices  17.6 us (6%)
  between operations  14.4 us (5%)
    reduce_scatter x1, waiting for transfers between devices, reduce_all(): return lax.psum_scatter(dw_stack, 'dp', scatter_dimension=3, tiled=True)  116 us
    ppermute x8, waiting for transfers between devices, partner_2(): return lax.ppermute(block, axis, route)  45.6 us
    dot_general x8, matrix products, weight_grad(): jnp.einsum('tbki,tbo->bkio', stacked, grad, preferred_element_type=jnp.fl...  20.8 us
    ppermute x8, starting transfers between devices, partner_2(): return lax.ppermute(block, axis, route)  17.6 us
    dot_general x8, matrix products, mix_level(): jnp.einsum('tbki,bkio->tbo', stacked, weight, preferred_element_type=jnp....  14.8 us
    dot_general x8, matrix products, back_terms(): jnp.einsum('tbo,bio->tbi', grad, weight[:, 1], preferred_element_type=jnp...  11 us
    dot_general x8, matrix products, back_terms(): jnp.einsum('tbo,bio->tbi', grad, weight[:, 0], preferred_element_type=jnp...  9.93 us
    rev x8, local copies, waits for them, and re-layouts, pair_flip(): return jnp.flip(r, 2).reshape(t, b, f)  8.41 us
  transfers between devices with their start and end apart: 9, of which 6 were waited for; matrix products, arithmetic and copies ran while one was open for 25% of the time, Pallas kernels for 0%

commit v1 on v0

v1 whole, which is shorter than its diff:
```python
import jax
import jax.numpy as jnp
from jax import lax
from jax.experimental import pallas as pl
from jax.experimental.pallas import tpu as pltpu
from jax.sharding import PartitionSpec as P

MESH = pl.DeviceIdType.MESH
BF = jnp.bfloat16
F32 = jnp.float32

S_X0, S_W, S_FZ, S_CA, S_XA, S_GA, S_MA, S_HA, S_TG, S_OB = range(10)
S_AG, S_CF, S_CD, S_RS, S_FS, N_SEM = 10, 14, 18, 26, 34, 42


def pair(q, d):
    return (q // d) * (2 * d) + q % d


def wide(a, b):
    return jnp.concatenate([a, b], axis=1)


def kernel(
    tok, fac, cot, mixed, tgrad, fgrad,
    xo, xt, go, gt, w, wt, csend, crecv, part, got, acc, fin, hs, hr, ob,
    rsem, ssem,
):
    dp, t = lax.axis_index("dp"), lax.axis_index("tensor")
    c, s = dp % 2, dp // 2
    oc = 1 - c
    xl, y = s // 4, s % 4

    def far(k):
        return (t + 8 + ((k + 1) // 2) * (1 - 2 * (k % 2))) % 16

    def chip(i):
        return ((xl + i // 4) % 2) * 4 + (y + i % 4) % 4

    def send(src, dst, slot, device):
        pltpu.make_async_remote_copy(
            src_ref=src, dst_ref=dst, send_sem=ssem.at[slot], recv_sem=rsem.at[slot],
            device_id=device, device_id_type=MESH,
        ).start()

    def local(src, dst, slot):
        pltpu.make_async_copy(src, dst, rsem.at[slot]).start()

    def arrived(ref, slot):
        pltpu.make_async_copy(ref, ref, rsem.at[slot]).wait()

    def left(ref, slot):
        pltpu.make_async_copy(ref, ref, ssem.at[slot]).wait()

    def loop(n, body, unroll=1):
        def step(i, carry):
            body(i)
            return carry

        lax.fori_loop(0, n, step, 0, unroll=unroll)

    sibling = (s * 2 + oc, t)

    def to_tensor(src, dst, slot):
        loop(15, lambda k: send(src(far(k)), dst, slot, (dp, far(k))))
        local(src(t), dst, slot)

    def to_chips(src, dst, slot):
        loop(7, lambda k: send(src(chip(k + 1)), dst, slot, (chip(k + 1) * 2 + c, t)))

    loop(16, lambda j: local(tok.at[:, pl.ds(pl.multiple_of(j * 128, 128), 128)], xo.at[0, j], S_X0))
    local(fac.at[pl.ds(0, 4)], w, S_W)

    barrier = pltpu.get_barrier_semaphore()

    def greet(device):
        pl.semaphore_signal(barrier, inc=1, device_id=device, device_id_type=MESH)

    loop(15, lambda k: greet((dp, far(k))))
    loop(7, lambda k: greet((chip(k + 1) * 2 + c, t)))
    greet(sibling)
    pl.semaphore_wait(barrier, 23)

    rows = pl.ds(pl.multiple_of(s * 16, 16), 16)
    to_tensor(lambda j: fac.at[pl.ds(4, 4), j, c, rows, :], wt.at[:, c, s, t], S_FZ)
    to_tensor(
        lambda j: cot.at[:, pl.ds(pl.multiple_of(j * 128, 128), 128)], gt.at[4, t], S_CA
    )

    def weights_low(level):
        return lambda b, k: w[level, b, k]

    def weights_high(lv):
        return lambda b, k: wt[lv, k, :, b].reshape(128, 128)

    def matrix(weights, b0, b1):
        return jnp.concatenate(
            [wide(weights(b0, 0), weights(b1, 1)), wide(weights(b0, 1), weights(b1, 0))], axis=0
        )

    def forward(x, at, d, weights):
        def body(q):
            b0 = pair(q, d)
            b1 = b0 + d
            new = jnp.dot(
                wide(x[at, b0], x[at, b1]), matrix(weights, b0, b1), preferred_element_type=F32
            ).astype(BF)
            x[at + 1, b0] = new[:, :128]
            x[at + 1, b1] = new[:, 128:]

        loop(8, body, 2)

    def backward(g, at, d, weights):
        def body(q):
            b0 = pair(q, d)
            b1 = b0 + d
            new = lax.dot_general(
                wide(g[at + 1, b0], g[at + 1, b1]), matrix(weights, b0, b1),
                (((1,), (1,)), ((), ())), preferred_element_type=F32,
            ).astype(BF)
            g[at, b0] = new[:, :128]
            g[at, b1] = new[:, 128:]

        loop(8, body, 2)

    def gradient(x, g, at, d, core, put):
        dl = min(d, 4)

        def body(q):
            b0 = pair(core * 4 + q, d)
            b1 = b0 + d
            dm = lax.dot_general(
                wide(x[at, b0], x[at, b1]), wide(g[at + 1, b0], g[at + 1, b1]),
                (((0,), (0,)), ((), ())), preferred_element_type=F32,
            )
            m0 = pair(q, dl)
            m1 = m0 + dl
            put(m0, 0, dm[:128, :128].reshape(8, 16, 128))
            put(m0, 1, dm[128:, :128].reshape(8, 16, 128))
            put(m1, 1, dm[:128, 128:].reshape(8, 16, 128))
            put(m1, 0, dm[128:, 128:].reshape(8, 16, 128))

        loop(4, body, 2)

    def side(level):
        return (xo, go, level) if level < 4 else (xt, gt, level - 4)

    def grad_out(level):
        x, g, at = side(level)

        def put(m, k, value):
            csend[level, :, m, k] = value.astype(BF)

        gradient(x, g, at, 2**at, oc, put)
        send(csend.at[level], crecv.at[level], S_CD + level, sibling)

    def grad_in(level):
        x, g, at = side(level)
        arrived(crecv.at[level], S_CD + level)

        def put(m, k, value):
            part[level, :, m, k] = (value + crecv[level, :, m, k].astype(F32)).astype(BF)

        gradient(x, g, at, 2**at, c, put)
        to_chips(lambda i: part.at[level, i], got.at[level, s], S_RS + level)
        local(part.at[level, s], got.at[level, s], S_RS + level)

    def finish(level, out, at):
        arrived(got.at[level], S_RS + level)

        def body(m):
            total = got[level, 0, m].astype(F32)
            for i in range(1, 8):
                total = total + got[level, i, m].astype(F32)
            acc[level, m] = total

        loop(8, body, 2)
        for u in range(2):
            first = 8 * c + 4 * u if level % 4 < 3 else 8 * u + 4 * c
            dst = out.at[at, pl.ds(first, 4)]
            mine = pl.ds(pl.multiple_of(c * 8, 8), 8)
            other = pl.ds(pl.multiple_of(oc * 8, 8), 8)
            local(acc.at[level, pl.ds(4 * u, 4), :, mine], dst, S_FS + level)
            send(acc.at[level, pl.ds(4 * u, 4), :, other], dst, S_FS + level, sibling)

    arrived(xo.at[0], S_X0)
    arrived(w, S_W)
    for level in range(4):
        forward(xo, level, 2**level, weights_low(level))
    to_tensor(lambda j: xo.at[4, j], xt.at[0, t], S_XA)

    arrived(wt.at[:, c, s], S_FZ)
    for lv in (3, 2, 1, 0):
        to_chips(lambda i, lv=lv: wt.at[lv, c, s], wt.at[lv, c, s], S_AG + lv)

    def pass_on(lv):
        arrived(wt.at[lv, c, pl.ds(0, 7)], S_AG + lv)
        send(wt.at[lv, c], wt.at[lv, c], S_CF + lv, sibling)

    pass_on(3)
    arrived(gt.at[4], S_CA)
    for lv in (3, 2, 1, 0):
        if lv > 0:
            pass_on(lv - 1)
        arrived(wt.at[lv, oc], S_CF + lv)
        backward(gt, lv, 2**lv, weights_high(lv))
    to_tensor(lambda j: gt.at[0, j], go.at[4, t], S_GA)

    arrived(xt.at[0], S_XA)
    for level in range(4, 8):
        grad_out(level)
        forward(xt, level - 4, 2 ** (level - 4), weights_high(level - 4))
        if level > 4:
            grad_in(level - 1)
    to_tensor(lambda j: xt.at[4, j], mixed.at[:, pl.ds(pl.multiple_of(t * 128, 128), 128)], S_MA)
    grad_in(7)

    arrived(go.at[4], S_GA)
    for level in (3, 2, 1, 0):
        grad_out(level)
        backward(go, level, 2**level, weights_low(level))
        if level < 3:
            grad_in(level + 1)
    loop(16, lambda j: local(go.at[0, j], tgrad.at[:, pl.ds(pl.multiple_of(j * 128, 128), 128)], S_TG))
    grad_in(0)

    for level in range(4, 8):
        finish(level, fin, level - 4)
    for level in range(4, 8):
        arrived(fin.at[level - 4], S_FS + level)

    def pack(h):
        for lv in range(4):
            hs[h, lv] = fin[lv, h].reshape(16, 128).astype(BF)

    loop(16, pack)
    to_tensor(lambda j: hs.at[j], hr.at[t], S_HA)

    for level in (3, 2, 1, 0):
        finish(level, fgrad, level)

    arrived(hr, S_HA)

    def unpack(j):
        for lv in range(4):
            ob[lv, j] = hr[j, lv].astype(F32).reshape(2, 8, 128)

    loop(16, unpack)
    local(ob, fgrad.at[pl.ds(4, 4)], S_OB)

    for level in range(4):
        arrived(fgrad.at[level], S_FS + level)
    arrived(mixed, S_MA)
    arrived(tgrad, S_TG)
    arrived(fgrad.at[pl.ds(4, 4)], S_OB)
    blocks = xo.at[0, pl.ds(0, 15)]
    for slot in (S_CA, S_XA, S_GA, S_MA):
        left(blocks, slot)
    left(hs.at[pl.ds(0, 15)], S_FZ)
    left(hs.at[pl.ds(0, 15)], S_HA)
    for lv in range(4):
        left(wt.at[lv, 0, pl.ds(0, 7)], S_AG + lv)
        left(wt.at[lv, 0], S_CF + lv)
    for level in range(8):
        left(csend.at[level], S_CD + level)
        left(part.at[level, pl.ds(0, 7)], S_RS + level)
        left(acc.at[level, :, :, pl.ds(0, 8)], S_FS + level)


def per_device(tokens, factors, cotangent):
    hbm = pl.BlockSpec(memory_space=pl.ANY)
    acts = pltpu.VMEM((5, 16, 128, 128), BF)
    grads = pltpu.VMEM((8, 8, 8, 2, 16, 128), BF)
    return pl.pallas_call(
        kernel,
        out_shape=(
            jax.ShapeDtypeStruct((128, 2048), BF),
            jax.ShapeDtypeStruct((128, 2048), BF),
            jax.ShapeDtypeStruct((8, 16, 2, 8, 128), F32),
        ),
        in_specs=[hbm] * 3,
        out_specs=[hbm] * 3,
        scratch_shapes=[
            acts, acts, acts, acts,
            pltpu.VMEM((4, 16, 2, 128, 128), BF),
            pltpu.VMEM((4, 2, 8, 16, 16, 128), BF),
            grads, grads, grads, grads,
            pltpu.VMEM((8, 8, 2, 16, 128), F32),
            pltpu.VMEM((4, 16, 2, 8, 128), F32),
            pltpu.VMEM((16, 4, 16, 128), BF),
            pltpu.VMEM((16, 4, 16, 128), BF),
            pltpu.VMEM((4, 16, 2, 8, 128), F32),
            pltpu.SemaphoreType.DMA((N_SEM,)),
            pltpu.SemaphoreType.DMA((N_SEM,)),
        ],
        compiler_params=pltpu.CompilerParams(
            collective_id=0, has_side_effects=True, vmem_limit_bytes=56 * 1024 * 1024
        ),
        cost_estimate=pl.CostEstimate(flops=3221225472, bytes_accessed=12582912, transcendentals=0),
        name="butterfly",
    )(tokens, factors, cotangent)


def solution(mesh):
    placed = (P("dp", "tensor"), P(None, "tensor", None, None, None), P("dp", "tensor"))
    return jax.shard_map(
        per_device,
        mesh=mesh,
        in_specs=placed,
        out_specs=(P("dp", "tensor"), P("dp", "tensor"), P(None, "tensor", None, "dp", None)),
        check_vma=False,
    )
```

time: 279 us -> 130 us (0.47)
  waiting for transfers between devices: 161 us -> 0 us
  Pallas kernels: 0 us -> 124 us
  matrix products: 56.5 us -> 0 us
  local copies, waits for them, and re-layouts: 26.9 us -> 6.03 us
  starting transfers between devices: 17.6 us -> 0 us
  between operations: 14.4 us -> 0.64 us
    pallas_call x0 -> x1, Pallas kernels: none -> 124 us  [per_device(): pl.pallas_call(kernel, out_shape=(jax.ShapeDtypeStruct((128, 2048), BF),...]
    reduce_scatter x1 -> x0, waiting for transfers between devices: 116 us -> none  [reduce_all(): return lax.psum_scatter(dw_stack, 'dp', scatter_dimension=3, tiled=True)]
    dot_general x32 -> x0, matrix products: 56.5 us -> none  [the longest x8 20.8 us: weight_grad(): jnp.einsum('tbki,tbo->bkio', stacked, grad, preferred_element_type=jnp.fl...]
    ppermute x8 -> x0, waiting for transfers between devices: 45.6 us -> none  [partner_2(): return lax.ppermute(block, axis, route)]
    ppermute x8 -> x0, starting transfers between devices: 17.6 us -> none  [partner_2(): return lax.ppermute(block, axis, route)]
    rev x8 -> x0, local copies, waits for them, and re-layouts: 8.41 us -> none  [pair_flip(): return jnp.flip(r, 2).reshape(t, b, f)]
    squeeze x1 -> x0, local copies, waits for them, and re-layouts: 5.79 us -> none  [per_device(): x = mix_level(x, partner, factors[level])]
    another operation x3 -> x0, local copies, waits for them, and re-layouts: 5.36 us -> none  [the longest x2 3.13 us: pair_flip(): r = x.reshape(t, b // (2 * dist), 2, dist, f)]
  transfers between devices with their start and end apart: 9 -> 0, of which waited for: 6 -> 0; matrix products, arithmetic and copies ran while one was open for 25% -> 0% of each run, Pallas kernels for 0% -> 0%
where the time goes in v1:
time: 130 us
  Pallas kernels  124 us (95%)
  local copies, waits for them, and re-layouts  6.03 us (5%)
    pallas_call x1, Pallas kernels, per_device(): pl.pallas_call(kernel, out_shape=(jax.ShapeDtypeStruct((128, 2048), BF),...  124 us
    unnamed x3, local copies, waits for them, and re-layouts  6.03 us

profile of v1, /device:TPU:1, one launch (start us, length us, event | category | flops | bytes accessed | tf_op | source)
XLA Modules:
  0.0 130.2 jit_solution(17359276542505306711)
XLA Ops:
  0.6 123.5 %butterfly.1 = (bf16[128,2048]{1,0:T(8,128)(2,1)}, bf16[128,2048]{1,0:T(8,128)(2,1)}, f32[8,16,2,8,128]{4,3,2,1,0:T(8,128)}) custom-call(bf16[128,2048]{1,0:T(8,128)(2,1)} %tok.1, bf16[8,16,2,128,128]{4,3,2,1,0:T(8,128)(2,1)} %fac.1, bf16[128,2048]{1,0:T(8,128)(2,1)} %cot.1), custom_call_target="tpu_custom_call" | custom-call | flops 3221225472 | bytes 12582912 | tf_op jit(solution)/shard_map/butterfly/pallas_call | solution.py:274
  124.2 1.9 %copy.9 = bf16[128,2048]{1,0:T(8,128)(2,1)} copy(bf16[128,2048]{1,0:T(8,128)(2,1)} %get-tuple-element.6) | data formatting | bytes 1048576
  126.0 1.9 %copy.10 = bf16[128,2048]{1,0:T(8,128)(2,1)} copy(bf16[128,2048]{1,0:T(8,128)(2,1)} %get-tuple-element.7) | data formatting | bytes 1048576
  127.9 2.3 %copy.11 = f32[8,16,2,8,128]{4,3,2,1,0:T(8,128)} copy(f32[8,16,2,8,128]{4,3,2,1,0:T(8,128)} %get-tuple-element.8) | data formatting | bytes 2097152

commit v2 on v1

--- a/solution.py
+++ b/solution.py
@@ -10,7 +10,7 @@
 F32 = jnp.float32
 
 S_X0, S_W, S_FZ, S_CA, S_XA, S_GA, S_MA, S_HA, S_TG, S_OB = range(10)
-S_AG, S_CF, S_CD, S_RS, S_FS, N_SEM = 10, 14, 18, 26, 34, 42
+S_AX, S_AY, S_CF, S_CD, S_RY, S_RX, S_FS, N_SEM = 10, 14, 18, 22, 30, 38, 46, 54
 
 
 def pair(q, d):
@@ -23,7 +23,7 @@
 
 def kernel(
     tok, fac, cot, mixed, tgrad, fgrad,
-    xo, xt, go, gt, w, wt, csend, crecv, part, got, acc, fin, hs, hr, ob,
+    xo, xt, go, gt, w, wt, csend, crecv, part, got, mid, other, acc, fin, hs, hr, ob,
     rsem, ssem,
 ):
     dp, t = lax.axis_index("dp"), lax.axis_index("tensor")
@@ -34,8 +34,8 @@
     def far(k):
         return (t + 8 + ((k + 1) // 2) * (1 - 2 * (k % 2))) % 16
 
-    def chip(i):
-        return ((xl + i // 4) % 2) * 4 + (y + i % 4) % 4
+    def along(i):
+        return (y + i) % 4
 
     def send(src, dst, slot, device):
         pltpu.make_async_remote_copy(
@@ -60,13 +60,15 @@
         lax.fori_loop(0, n, step, 0, unroll=unroll)
 
     sibling = (s * 2 + oc, t)
+    across = ((s + 4) % 8 * 2 + c, t)
 
     def to_tensor(src, dst, slot):
         loop(15, lambda k: send(src(far(k)), dst, slot, (dp, far(k))))
         local(src(t), dst, slot)
 
-    def to_chips(src, dst, slot):
-        loop(7, lambda k: send(src(chip(k + 1)), dst, slot, (chip(k + 1) * 2 + c, t)))
+    def to_row(src, dst, slot):
+        for i in (2, 1, 3):
+            send(src(along(i)), dst, slot, ((xl * 4 + along(i)) * 2 + c, t))
 
     loop(16, lambda j: local(tok.at[:, pl.ds(pl.multiple_of(j * 128, 128), 128)], xo.at[0, j], S_X0))
     local(fac.at[pl.ds(0, 4)], w, S_W)
@@ -77,12 +79,14 @@
         pl.semaphore_signal(barrier, inc=1, device_id=device, device_id_type=MESH)
 
     loop(15, lambda k: greet((dp, far(k))))
-    loop(7, lambda k: greet((chip(k + 1) * 2 + c, t)))
+    for i in (1, 2, 3):
+        greet(((xl * 4 + along(i)) * 2 + c, t))
+    greet(across)
     greet(sibling)
-    pl.semaphore_wait(barrier, 23)
+    pl.semaphore_wait(barrier, 20)
 
     rows = pl.ds(pl.multiple_of(s * 16, 16), 16)
-    to_tensor(lambda j: fac.at[pl.ds(4, 4), j, c, rows, :], wt.at[:, c, s, t], S_FZ)
+    to_tensor(lambda j: fac.at[pl.ds(4, 4), j, c, rows, :], wt.at[:, c, xl, y, t], S_FZ)
     to_tensor(
         lambda j: cot.at[:, pl.ds(pl.multiple_of(j * 128, 128), 128)], gt.at[4, t], S_CA
     )
@@ -91,7 +95,7 @@
         return lambda b, k: w[level, b, k]
 
     def weights_high(lv):
-        return lambda b, k: wt[lv, k, :, b].reshape(128, 128)
+        return lambda b, k: wt[lv, k, :, :, b].reshape(128, 128)
 
     def matrix(weights, b0, b1):
         return jnp.concatenate(
@@ -108,7 +112,7 @@
             x[at + 1, b0] = new[:, :128]
             x[at + 1, b1] = new[:, 128:]
 
-        loop(8, body, 2)
+        loop(8, body, 8)
 
     def backward(g, at, d, weights):
         def body(q):
@@ -121,7 +125,7 @@
             g[at, b0] = new[:, :128]
             g[at, b1] = new[:, 128:]
 
-        loop(8, body, 2)
+        loop(8, body, 8)
 
     def gradient(x, g, at, d, core, put):
         dl = min(d, 4)
@@ -135,12 +139,12 @@
             )
             m0 = pair(q, dl)
             m1 = m0 + dl
-            put(m0, 0, dm[:128, :128].reshape(8, 16, 128))
-            put(m0, 1, dm[128:, :128].reshape(8, 16, 128))
-            put(m1, 1, dm[:128, 128:].reshape(8, 16, 128))
-            put(m1, 0, dm[128:, 128:].reshape(8, 16, 128))
-
-        loop(4, body, 2)
+            put(m0, 0, dm[:128, :128].reshape(2, 4, 16, 128))
+            put(m0, 1, dm[128:, :128].reshape(2, 4, 16, 128))
+            put(m1, 1, dm[:128, 128:].reshape(2, 4, 16, 128))
+            put(m1, 0, dm[128:, 128:].reshape(2, 4, 16, 128))
+
+        loop(4, body, 4)
 
     def side(level):
         return (xo, go, level) if level < 4 else (xt, gt, level - 4)
@@ -149,7 +153,7 @@
         x, g, at = side(level)
 
         def put(m, k, value):
-            csend[level, :, m, k] = value.astype(BF)
+            csend[level, :, :, m, k] = value.astype(BF)
 
         gradient(x, g, at, 2**at, oc, put)
         send(csend.at[level], crecv.at[level], S_CD + level, sibling)
@@ -159,46 +163,67 @@
         arrived(crecv.at[level], S_CD + level)
 
         def put(m, k, value):
-            part[level, :, m, k] = (value + crecv[level, :, m, k].astype(F32)).astype(BF)
+            part[level, :, :, m, k] = (value + crecv[level, :, :, m, k].astype(F32)).astype(BF)
 
         gradient(x, g, at, 2**at, c, put)
-        to_chips(lambda i: part.at[level, i], got.at[level, s], S_RS + level)
-        local(part.at[level, s], got.at[level, s], S_RS + level)
+        to_row(lambda i: part.at[level, :, i], got.at[level, :, y], S_RY + level)
+
+    def gather(level):
+        arrived(got.at[level, :, pl.ds(0, 3)], S_RY + level)
+
+        def total(side_of, m):
+            value = part[level, side_of, y, m].astype(F32)
+            for i in (1, 2, 3):
+                value = value + got[level, side_of, along(i), m].astype(F32)
+            return value
+
+        def give(m):
+            mid[level, m] = total(1 - xl, m).astype(BF)
+
+        def keep(m):
+            acc[level, m] = total(xl, m)
+
+        loop(8, give, 4)
+        send(mid.at[level], other.at[level], S_RX + level, across)
+        loop(8, keep, 4)
 
     def finish(level, out, at):
-        arrived(got.at[level], S_RS + level)
+        arrived(other.at[level], S_RX + level)
 
         def body(m):
-            total = got[level, 0, m].astype(F32)
-            for i in range(1, 8):
-                total = total + got[level, i, m].astype(F32)
-            acc[level, m] = total
-
-        loop(8, body, 2)
+            acc[level, m] = acc[level, m] + other[level, m].astype(F32)
+
+        loop(8, body, 4)
         for u in range(2):
             first = 8 * c + 4 * u if level % 4 < 3 else 8 * u + 4 * c
             dst = out.at[at, pl.ds(first, 4)]
             mine = pl.ds(pl.multiple_of(c * 8, 8), 8)
-            other = pl.ds(pl.multiple_of(oc * 8, 8), 8)
+            theirs = pl.ds(pl.multiple_of(oc * 8, 8), 8)
             local(acc.at[level, pl.ds(4 * u, 4), :, mine], dst, S_FS + level)
-            send(acc.at[level, pl.ds(4 * u, 4), :, other], dst, S_FS + level, sibling)
+            send(acc.at[level, pl.ds(4 * u, 4), :, theirs], dst, S_FS + level, sibling)
 
     arrived(xo.at[0], S_X0)
     arrived(w, S_W)
     for level in range(4):
         forward(xo, level, 2**level, weights_low(level))
-    to_tensor(lambda j: xo.at[4, j], xt.at[0, t], S_XA)
-
-    arrived(wt.at[:, c, s], S_FZ)
+
+    arrived(wt.at[:, c, xl, y], S_FZ)
     for lv in (3, 2, 1, 0):
-        to_chips(lambda i, lv=lv: wt.at[lv, c, s], wt.at[lv, c, s], S_AG + lv)
+        piece = wt.at[lv, c, xl, y]
+        send(piece, piece, S_AX + lv, across)
+        to_row(lambda i, piece=piece: piece, piece, S_AY + lv)
+    for lv in (3, 2, 1, 0):
+        piece = wt.at[lv, c, 1 - xl, y]
+        arrived(piece, S_AX + lv)
+        to_row(lambda i, piece=piece: piece, piece, S_AY + lv)
 
     def pass_on(lv):
-        arrived(wt.at[lv, c, pl.ds(0, 7)], S_AG + lv)
+        arrived(wt.at[lv, c, :, pl.ds(0, 3)], S_AY + lv)
         send(wt.at[lv, c], wt.at[lv, c], S_CF + lv, sibling)
 
     pass_on(3)
     arrived(gt.at[4], S_CA)
+    to_tensor(lambda j: xo.at[4, j], xt.at[0, t], S_XA)
     for lv in (3, 2, 1, 0):
         if lv > 0:
             pass_on(lv - 1)
@@ -215,6 +240,8 @@
     to_tensor(lambda j: xt.at[4, j], mixed.at[:, pl.ds(pl.multiple_of(t * 128, 128), 128)], S_MA)
     grad_in(7)
 
+    gather(4)
+
     arrived(go.at[4], S_GA)
     for level in (3, 2, 1, 0):
         grad_out(level)
@@ -224,6 +251,8 @@
     loop(16, lambda j: local(go.at[0, j], tgrad.at[:, pl.ds(pl.multiple_of(j * 128, 128), 128)], S_TG))
     grad_in(0)
 
+    for level in range(5, 8):
+        gather(level)
     for level in range(4, 8):
         finish(level, fin, level - 4)
     for level in range(4, 8):
@@ -236,6 +265,8 @@
     loop(16, pack)
     to_tensor(lambda j: hs.at[j], hr.at[t], S_HA)
 
+    for level in (3, 2, 1, 0):
+        gather(level)
     for level in (3, 2, 1, 0):
         finish(level, fgrad, level)
 
@@ -259,18 +290,21 @@
     left(hs.at[pl.ds(0, 15)], S_FZ)
     left(hs.at[pl.ds(0, 15)], S_HA)
     for lv in range(4):
-        left(wt.at[lv, 0, pl.ds(0, 7)], S_AG + lv)
+        left(wt.at[lv, 0, 0, 0], S_AX + lv)
+        left(wt.at[lv, 0, :, pl.ds(0, 3)], S_AY + lv)
         left(wt.at[lv, 0], S_CF + lv)
     for level in range(8):
         left(csend.at[level], S_CD + level)
-        left(part.at[level, pl.ds(0, 7)], S_RS + level)
+        left(part.at[level, :, pl.ds(0, 3)], S_RY + level)
+        left(mid.at[level], S_RX + level)
         left(acc.at[level, :, :, pl.ds(0, 8)], S_FS + level)
 
 
 def per_device(tokens, factors, cotangent):
     hbm = pl.BlockSpec(memory_space=pl.ANY)
     acts = pltpu.VMEM((5, 16, 128, 128), BF)
-    grads = pltpu.VMEM((8, 8, 8, 2, 16, 128), BF)
+    grads = pltpu.VMEM((8, 2, 4, 8, 2, 16, 128), BF)
+    slab = pltpu.VMEM((8, 8, 2, 16, 128), BF)
     return pl.pallas_call(
         kernel,
         out_shape=(
@@ -283,8 +317,8 @@
         scratch_shapes=[
             acts, acts, acts, acts,
             pltpu.VMEM((4, 16, 2, 128, 128), BF),
-            pltpu.VMEM((4, 2, 8, 16, 16, 128), BF),
-            grads, grads, grads, grads,
+            pltpu.VMEM((4, 2, 2, 4, 16, 16, 128), BF),
+            grads, grads, grads, grads, slab, slab,
             pltpu.VMEM((8, 8, 2, 16, 128), F32),
             pltpu.VMEM((4, 16, 2, 8, 128), F32),
             pltpu.VMEM((16, 4, 16, 128), BF),

time: 130 us -> 111 us (0.85)
  Pallas kernels: 124 us -> 104 us
    pallas_call x1, Pallas kernels: 124 us -> 104 us  [per_device(): pl.pallas_call(kernel, out_shape=(jax.ShapeDtypeStruct((128, 2048), BF),...]
where the time goes in v2:
time: 111 us; the launch traced here: 110 us
  Pallas kernels  104 us (94%)
  local copies, waits for them, and re-layouts  6.03 us (5%)
    pallas_call x1, Pallas kernels, per_device(): pl.pallas_call(kernel, out_shape=(jax.ShapeDtypeStruct((128, 2048), BF),...  104 us
    unnamed x3, local copies, waits for them, and re-layouts  6.03 us

profile of v2, /device:TPU:1, one launch (start us, length us, event | category | flops | bytes accessed | tf_op | source)
XLA Modules:
  0.0 110.4 jit_solution(9695452436951918753)
XLA Ops:
  0.6 103.8 %butterfly.1 = (bf16[128,2048]{1,0:T(8,128)(2,1)}, bf16[128,2048]{1,0:T(8,128)(2,1)}, f32[8,16,2,8,128]{4,3,2,1,0:T(8,128)}) custom-call(bf16[128,2048]{1,0:T(8,128)(2,1)} %tok.1, bf16[8,16,2,128,128]{4,3,2,1,0:T(8,128)(2,1)} %fac.1, bf16[128,2048]{1,0:T(8,128)(2,1)} %cot.1), custom_call_target="tpu_custom_call" | custom-call | flops 3221225472 | bytes 12582912 | tf_op jit(solution)/shard_map/butterfly/pallas_call | solution.py:308
  104.4 1.9 %copy.9 = bf16[128,2048]{1,0:T(8,128)(2,1)} copy(bf16[128,2048]{1,0:T(8,128)(2,1)} %get-tuple-element.6) | data formatting | bytes 1048576
  106.3 1.9 %copy.10 = bf16[128,2048]{1,0:T(8,128)(2,1)} copy(bf16[128,2048]{1,0:T(8,128)(2,1)} %get-tuple-element.7) | data formatting | bytes 1048576
  108.2 2.3 %copy.11 = f32[8,16,2,8,128]{4,3,2,1,0:T(8,128)} copy(f32[8,16,2,8,128]{4,3,2,1,0:T(8,128)} %get-tuple-element.8) | data formatting | bytes 2097152

commit v3 on v2

--- a/solution.py
+++ b/solution.py
@@ -10,7 +10,8 @@
 F32 = jnp.float32
 
 S_X0, S_W, S_FZ, S_CA, S_XA, S_GA, S_MA, S_HA, S_TG, S_OB = range(10)
-S_AX, S_AY, S_CF, S_CD, S_RY, S_RX, S_FS, N_SEM = 10, 14, 18, 22, 30, 38, 46, 54
+S_AX, S_AY, S_AR, S_CF, S_CD, S_RR, S_RY, S_RX, S_FS = 10, 14, 18, 22, 26, 34, 42, 50, 58
+S_FY, N_SEM = 66, 67
 
 
 def pair(q, d):
@@ -23,7 +24,7 @@
 
 def kernel(
     tok, fac, cot, mixed, tgrad, fgrad,
-    xo, xt, go, gt, w, wt, csend, crecv, part, got, mid, other, acc, fin, hs, hr, ob,
+    xo, xt, go, gt, w, wt, csend, crecv, part, rel, rsum, got, mid, other, acc, fin, hs, hr, ob,
     rsem, ssem,
 ):
     dp, t = lax.axis_index("dp"), lax.axis_index("tensor")
@@ -66,27 +67,28 @@
         loop(15, lambda k: send(src(far(k)), dst, slot, (dp, far(k))))
         local(src(t), dst, slot)
 
-    def to_row(src, dst, slot):
-        for i in (2, 1, 3):
-            send(src(along(i)), dst, slot, ((xl * 4 + along(i)) * 2 + c, t))
-
+    up, down = along(1), along(3)
+    above = ((xl * 4 + up) * 2 + c, t)
+    below = ((xl * 4 + down) * 2 + c, t)
+
+    barrier = pltpu.get_barrier_semaphore()
+
+    def greet(device):
+        pl.semaphore_signal(barrier, inc=1, device_id=device, device_id_type=MESH)
+
+    loop(15, lambda k: greet((dp, far(k))))
+    greet(above)
+    greet(below)
+    greet(across)
+    greet(sibling)
     loop(16, lambda j: local(tok.at[:, pl.ds(pl.multiple_of(j * 128, 128), 128)], xo.at[0, j], S_X0))
     local(fac.at[pl.ds(0, 4)], w, S_W)
 
-    barrier = pltpu.get_barrier_semaphore()
-
-    def greet(device):
-        pl.semaphore_signal(barrier, inc=1, device_id=device, device_id_type=MESH)
-
-    loop(15, lambda k: greet((dp, far(k))))
-    for i in (1, 2, 3):
-        greet(((xl * 4 + along(i)) * 2 + c, t))
-    greet(across)
-    greet(sibling)
-    pl.semaphore_wait(barrier, 20)
+    pl.semaphore_wait(barrier, 19)
 
     rows = pl.ds(pl.multiple_of(s * 16, 16), 16)
-    to_tensor(lambda j: fac.at[pl.ds(4, 4), j, c, rows, :], wt.at[:, c, xl, y, t], S_FZ)
+    to_tensor(lambda j: fac.at[7, j, c, rows, :], wt.at[3, c, xl, y, t], S_FZ)
+    to_tensor(lambda j: fac.at[pl.ds(4, 3), j, c, rows, :], wt.at[pl.ds(0, 3), c, xl, y, t], S_FY)
     to_tensor(
         lambda j: cot.at[:, pl.ds(pl.multiple_of(j * 128, 128), 128)], gt.at[4, t], S_CA
     )
@@ -166,15 +168,30 @@
             part[level, :, :, m, k] = (value + crecv[level, :, :, m, k].astype(F32)).astype(BF)
 
         gradient(x, g, at, 2**at, c, put)
-        to_row(lambda i: part.at[level, :, i], got.at[level, :, y], S_RY + level)
+        send(part.at[level, 0, along(2)], rel.at[level, 0], S_RR + level, above)
+        send(part.at[level, 1, along(2)], rel.at[level, 1], S_RR + level, below)
+        send(part.at[level, 1, up], got.at[level, 1, 0], S_RY + level, above)
+        send(part.at[level, 0, down], got.at[level, 0, 0], S_RY + level, below)
+
+    def relay(level):
+        arrived(rel.at[level], S_RR + level)
+
+        def body(m):
+            for u, way in ((0, up), (1, down)):
+                value = rel[level, u, m].astype(F32) + part[level, u, way, m].astype(F32)
+                rsum[level, u, m] = value.astype(BF)
+
+        loop(8, body, 4)
+        send(rsum.at[level, 0], got.at[level, 0, 1], S_RY + level, above)
+        send(rsum.at[level, 1], got.at[level, 1, 1], S_RY + level, below)
 
     def gather(level):
-        arrived(got.at[level, :, pl.ds(0, 3)], S_RY + level)
+        arrived(got.at[level], S_RY + level)
 
         def total(side_of, m):
             value = part[level, side_of, y, m].astype(F32)
-            for i in (1, 2, 3):
-                value = value + got[level, side_of, along(i), m].astype(F32)
+            for i in range(2):
+                value = value + got[level, side_of, i, m].astype(F32)
             return value
 
         def give(m):
@@ -207,24 +224,47 @@
     for level in range(4):
         forward(xo, level, 2**level, weights_low(level))
 
-    arrived(wt.at[:, c, xl, y], S_FZ)
-    for lv in (3, 2, 1, 0):
+    to_tensor(lambda j: xo.at[4, j], xt.at[0, t], S_XA)
+
+    def share(lv):
         piece = wt.at[lv, c, xl, y]
         send(piece, piece, S_AX + lv, across)
-        to_row(lambda i, piece=piece: piece, piece, S_AY + lv)
-    for lv in (3, 2, 1, 0):
+        send(piece, piece, S_AY + lv, above)
+        send(piece, piece, S_AY + lv, below)
+
+    def share_more(lv):
         piece = wt.at[lv, c, 1 - xl, y]
         arrived(piece, S_AX + lv)
-        to_row(lambda i, piece=piece: piece, piece, S_AY + lv)
+        send(piece, piece, S_AY + lv, above)
+        send(piece, piece, S_AY + lv, below)
+
+    def share_on(lv):
+        arrived(wt.at[lv, c, :, pl.ds(0, 2)], S_AY + lv)
+        first, second = wt.at[lv, c, 0, down], wt.at[lv, c, 1, up]
+        send(first, first, S_AR + lv, above)
+        send(second, second, S_AR + lv, below)
 
     def pass_on(lv):
-        arrived(wt.at[lv, c, :, pl.ds(0, 3)], S_AY + lv)
+        arrived(wt.at[lv, c, :, 0], S_AR + lv)
         send(wt.at[lv, c], wt.at[lv, c], S_CF + lv, sibling)
 
+    arrived(wt.at[0, c, xl, y], S_FZ)
+    share(3)
+    arrived(wt.at[pl.ds(0, 3), c, xl, y], S_FY)
+    share(2)
+    share_more(3)
+    share(1)
+    share(0)
+    share_more(2)
+    share_on(3)
+    share_more(1)
+    share_more(0)
+    share_on(2)
     pass_on(3)
     arrived(gt.at[4], S_CA)
-    to_tensor(lambda j: xo.at[4, j], xt.at[0, t], S_XA)
     for lv in (3, 2, 1, 0):
+        if lv > 1:
+            share_on(lv - 2)
         if lv > 0:
             pass_on(lv - 1)
         arrived(wt.at[lv, oc], S_CF + lv)
@@ -237,22 +277,24 @@
         forward(xt, level - 4, 2 ** (level - 4), weights_high(level - 4))
         if level > 4:
             grad_in(level - 1)
+        if level > 5:
+            relay(level - 2)
     to_tensor(lambda j: xt.at[4, j], mixed.at[:, pl.ds(pl.multiple_of(t * 128, 128), 128)], S_MA)
     grad_in(7)
 
+    relay(6)
     gather(4)
 
     arrived(go.at[4], S_GA)
     for level in (3, 2, 1, 0):
         grad_out(level)
         backward(go, level, 2**level, weights_low(level))
-        if level < 3:
-            grad_in(level + 1)
+        grad_in(level)
+        relay(7 if level == 3 else level + 1)
+        if level > 0:
+            gather(8 - level)
     loop(16, lambda j: local(go.at[0, j], tgrad.at[:, pl.ds(pl.multiple_of(j * 128, 128), 128)], S_TG))
-    grad_in(0)
-
-    for level in range(5, 8):
-        gather(level)
+
     for level in range(4, 8):
         finish(level, fin, level - 4)
     for level in range(4, 8):
@@ -265,10 +307,15 @@
     loop(16, pack)
     to_tensor(lambda j: hs.at[j], hr.at[t], S_HA)
 
-    for level in (3, 2, 1, 0):
-        gather(level)
-    for level in (3, 2, 1, 0):
-        finish(level, fgrad, level)
+    gather(3)
+    relay(0)
+    gather(2)
+    finish(3, fgrad, 3)
+    gather(1)
+    finish(2, fgrad, 2)
+    gather(0)
+    finish(1, fgrad, 1)
+    finish(0, fgrad, 0)
 
     arrived(hr, S_HA)
 
@@ -287,17 +334,33 @@
     blocks = xo.at[0, pl.ds(0, 15)]
     for slot in (S_CA, S_XA, S_GA, S_MA):
         left(blocks, slot)
-    left(hs.at[pl.ds(0, 15)], S_FZ)
+    left(hs.at[pl.ds(0, 15), 0], S_FZ)
+    left(hs.at[pl.ds(0, 15), pl.ds(0, 3)], S_FY)
     left(hs.at[pl.ds(0, 15)], S_HA)
     for lv in range(4):
         left(wt.at[lv, 0, 0, 0], S_AX + lv)
-        left(wt.at[lv, 0, :, pl.ds(0, 3)], S_AY + lv)
+        left(wt.at[lv, 0, :, pl.ds(0, 2)], S_AY + lv)
+        left(wt.at[lv, 0, :, 0], S_AR + lv)
         left(wt.at[lv, 0], S_CF + lv)
     for level in range(8):
         left(csend.at[level], S_CD + level)
-        left(part.at[level, :, pl.ds(0, 3)], S_RY + level)
+        left(rel.at[level], S_RR + level)
+        left(got.at[level], S_RY + level)
         left(mid.at[level], S_RX + level)
         left(acc.at[level, :, :, pl.ds(0, 8)], S_FS + level)
+
+
+def hand_over(a, b, c, a_out, b_out, c_out, a_held, b_held, c_held, sem):
+    moves = ((c, c_held, c_out), (a, a_held, a_out), (b, b_held, b_out))
+    into = [pltpu.make_async_copy(m[0], m[1], sem.at[i]) for i, m in enumerate(moves)]
+    out = [pltpu.make_async_copy(m[1], m[2], sem.at[3 + i]) for i, m in enumerate(moves)]
+    for copy in into:
+        copy.start()
+    for i in range(3):
+        into[i].wait()
+        out[i].start()
+    for copy in out:
+        copy.wait()
 
 
 def per_device(tokens, factors, cotangent):
@@ -305,20 +368,22 @@
     acts = pltpu.VMEM((5, 16, 128, 128), BF)
     grads = pltpu.VMEM((8, 2, 4, 8, 2, 16, 128), BF)
     slab = pltpu.VMEM((8, 8, 2, 16, 128), BF)
-    return pl.pallas_call(
+    two = pltpu.VMEM((8, 2, 8, 2, 16, 128), BF)
+    shapes = (
+        jax.ShapeDtypeStruct((128, 2048), BF),
+        jax.ShapeDtypeStruct((128, 2048), BF),
+        jax.ShapeDtypeStruct((8, 16, 2, 8, 128), F32),
+    )
+    results = pl.pallas_call(
         kernel,
-        out_shape=(
-            jax.ShapeDtypeStruct((128, 2048), BF),
-            jax.ShapeDtypeStruct((128, 2048), BF),
-            jax.ShapeDtypeStruct((8, 16, 2, 8, 128), F32),
-        ),
+        out_shape=shapes,
         in_specs=[hbm] * 3,
         out_specs=[hbm] * 3,
         scratch_shapes=[
             acts, acts, acts, acts,
             pltpu.VMEM((4, 16, 2, 128, 128), BF),
             pltpu.VMEM((4, 2, 2, 4, 16, 16, 128), BF),
-            grads, grads, grads, grads, slab, slab,
+            grads, grads, grads, two, two, pltpu.VMEM((8, 2, 2, 8, 2, 16, 128), BF), slab, slab,
             pltpu.VMEM((8, 8, 2, 16, 128), F32),
             pltpu.VMEM((4, 16, 2, 8, 128), F32),
             pltpu.VMEM((16, 4, 16, 128), BF),
@@ -333,6 +398,14 @@
         cost_estimate=pl.CostEstimate(flops=3221225472, bytes_accessed=12582912, transcendentals=0),
         name="butterfly",
     )(tokens, factors, cotangent)
+    return pl.pallas_call(
+        hand_over,
+        out_shape=shapes,
+        in_specs=[hbm] * 3,
+        out_specs=[hbm] * 3,
+        scratch_shapes=[pltpu.VMEM(x.shape, x.dtype) for x in shapes] + [pltpu.SemaphoreType.DMA((6,))],
+        name="hand_over",
+    )(*results)
 
 
 def solution(mesh):

time: 111 us -> 91.4 us (0.82)
  Pallas kernels: 104 us -> 90.7 us
  local copies, waits for them, and re-layouts: 6.03 us -> 0 us
    pallas_call x1 -> x2, Pallas kernels: 104 us -> 90.7 us  [the longest x1 88.1 us: per_device(): pl.pallas_call(kernel, out_shape=shapes, in_specs=[hbm] * 3, out_specs=[h...]
    unnamed x3 -> x0, local copies, waits for them, and re-layouts: 6.03 us -> none
where the time goes in v3:
time: 91.4 us; the launch traced here: 91.3 us
  Pallas kernels  90.7 us (99%)
    pallas_call x1, Pallas kernels, per_device(): pl.pallas_call(kernel, out_shape=shapes, in_specs=[hbm] * 3, out_specs=[h...  88.1 us
    pallas_call x1, Pallas kernels, per_device(): pl.pallas_call(hand_over, out_shape=shapes, in_specs=[hbm] * 3, out_specs...  2.59 us

profile of v3, /device:TPU:1, one launch (start us, length us, event | category | flops | bytes accessed | tf_op | source)
XLA Modules:
  0.0 91.3 jit_solution(13472310731550466047)
XLA Ops:
  0.6 88.1 %butterfly.1 = (bf16[128,2048]{1,0:T(8,128)(2,1)}, bf16[128,2048]{1,0:T(8,128)(2,1)}, f32[8,16,2,8,128]{4,3,2,1,0:T(8,128)}) custom-call(bf16[128,2048]{1,0:T(8,128)(2,1)} %tok.1, bf16[8,16,2,128,128]{4,3,2,1,0:T(8,128)(2,1)} %fac.1, bf16[128,2048]{1,0:T(8,128)(2,1)} %cot.1), custom_call_target="tpu_custom_call" | custom-call | flops 3221225472 | bytes 12582912 | tf_op jit(solution)/shard_map/butterfly/pallas_call | solution.py:377
  88.7 2.6 %hand_over.1 = (bf16[128,2048]{1,0:T(8,128)(2,1)}, bf16[128,2048]{1,0:T(8,128)(2,1)}, f32[8,16,2,8,128]{4,3,2,1,0:T(8,128)}) custom-call(bf16[128,2048]{1,0:T(8,128)(2,1)} %get-tuple-element.6.a, bf16[128,2048]{1,0:T(8,128)(2,1)} %get-tuple-element.7.b, f32[8,16,2,8,128]{4,3,2,1,0:T(8,128)} %get-tuple-element.8.c), custom_call_target="tpu_custom_call" | custom-call | tf_op jit(solution)/shard_map/hand_over/pallas_call | solution.py:401

commit v4 on v3

--- a/solution.py
+++ b/solution.py
@@ -11,7 +11,14 @@
 
 S_X0, S_W, S_FZ, S_CA, S_XA, S_GA, S_MA, S_HA, S_TG, S_OB = range(10)
 S_AX, S_AY, S_AR, S_CF, S_CD, S_RR, S_RY, S_RX, S_FS = 10, 14, 18, 22, 26, 34, 42, 50, 58
-S_FY, N_SEM = 66, 67
+S_FY, S_HB, S_OC, N_SEM = 66, 67, 68, 69
+ACROSS_FIRST = ()
+ORDER = (
+    "o4", "f4", "o5", "f5", "i4", "o6", "f6", "i5", "r4", "o7", "f7", "i6", "r5", "M0",
+    "i7", "r6", "g4", "G0", "o3", "b3", "i3", "r7", "g5", "o2", "b2", "i2", "r3", "g6",
+    "e4", "e5", "o1", "b1", "i1", "r2", "g7", "H0", "o0", "b0", "i0", "e6", "e7", "r1",
+    "T0", "H1", "g3", "r0", "g2", "e3", "g1", "e2", "I0", "g0", "e1", "I1", "e0",
+)
 
 
 def pair(q, d):
@@ -24,7 +31,7 @@
 
 def kernel(
     tok, fac, cot, mixed, tgrad, fgrad,
-    xo, xt, go, gt, w, wt, csend, crecv, part, rel, rsum, got, mid, other, acc, fin, hs, hr, ob,
+    xo, xt, go, gt, w, wt, csend, crecv, part, rel, rsum, got, mid, other, xin, acc, fin, hs, hr, ob,
     rsem, ssem,
 ):
     dp, t = lax.axis_index("dp"), lax.axis_index("tensor")
@@ -66,6 +73,9 @@
     def to_tensor(src, dst, slot):
         loop(15, lambda k: send(src(far(k)), dst, slot, (dp, far(k))))
         local(src(t), dst, slot)
+
+    def span(level):
+        return 4 if level in ACROSS_FIRST else 8
 
     up, down = along(1), along(3)
     above = ((xl * 4 + up) * 2 + c, t)
@@ -87,6 +97,7 @@
     pl.semaphore_wait(barrier, 19)
 
     rows = pl.ds(pl.multiple_of(s * 16, 16), 16)
+
     to_tensor(lambda j: fac.at[7, j, c, rows, :], wt.at[3, c, xl, y, t], S_FZ)
     to_tensor(lambda j: fac.at[pl.ds(4, 3), j, c, rows, :], wt.at[pl.ds(0, 3), c, xl, y, t], S_FY)
     to_tensor(
@@ -168,49 +179,93 @@
             part[level, :, :, m, k] = (value + crecv[level, :, :, m, k].astype(F32)).astype(BF)
 
         gradient(x, g, at, 2**at, c, put)
-        send(part.at[level, 0, along(2)], rel.at[level, 0], S_RR + level, above)
-        send(part.at[level, 1, along(2)], rel.at[level, 1], S_RR + level, below)
-        send(part.at[level, 1, up], got.at[level, 1, 0], S_RY + level, above)
-        send(part.at[level, 0, down], got.at[level, 0, 0], S_RY + level, below)
+        if level in ACROSS_FIRST:
+            send(part.at[level, 1 - xl], xin.at[level], S_RX + level, across)
+        else:
+            set_off(level)
+
+    def ways(level):
+        return ((xl, 0), (xl, 4)) if level in ACROSS_FIRST else ((0, 0), (1, 0))
+
+    def set_off(level):
+        n = span(level)
+        (us, um), (ds, dm) = ways(level)
+        head = pl.ds(0, n)
+
+        def piece(side_of, way, first):
+            return part.at[level, side_of, way, pl.ds(first, n)]
+
+        send(piece(us, along(2), um), rel.at[level, 0, head], S_RR + level, above)
+        send(piece(ds, along(2), dm), rel.at[level, 1, head], S_RR + level, below)
+        send(piece(ds, up, dm), got.at[level, 1, 0, head], S_RY + level, above)
+        send(piece(us, down, um), got.at[level, 0, 0, head], S_RY + level, below)
+
+    def meet(level):
+        if level not in ACROSS_FIRST:
+            return
+        arrived(xin.at[level], S_RX + level)
+
+        def body(m):
+            for i in range(4):
+                value = part[level, xl, i, m].astype(F32) + xin[level, i, m].astype(F32)
+                part[level, xl, i, m] = value.astype(BF)
+
+        loop(8, body, 4)
+        set_off(level)
 
     def relay(level):
-        arrived(rel.at[level], S_RR + level)
+        n = span(level)
+        (us, um), (ds, dm) = ways(level)
+        head = pl.ds(0, n)
+        arrived(rel.at[level, :, head], S_RR + level)
 
         def body(m):
-            for u, way in ((0, up), (1, down)):
-                value = rel[level, u, m].astype(F32) + part[level, u, way, m].astype(F32)
-                rsum[level, u, m] = value.astype(BF)
-
-        loop(8, body, 4)
-        send(rsum.at[level, 0], got.at[level, 0, 1], S_RY + level, above)
-        send(rsum.at[level, 1], got.at[level, 1, 1], S_RY + level, below)
+            first = rel[level, 0, m].astype(F32) + part[level, us, up, um + m].astype(F32)
+            second = rel[level, 1, m].astype(F32) + part[level, ds, down, dm + m].astype(F32)
+            rsum[level, 0, m] = first.astype(BF)
+            rsum[level, 1, m] = second.astype(BF)
+
+        loop(n, body, 4)
+        send(rsum.at[level, 0, head], got.at[level, 0, 1, head], S_RY + level, above)
+        send(rsum.at[level, 1, head], got.at[level, 1, 1, head], S_RY + level, below)
 
     def gather(level):
-        arrived(got.at[level], S_RY + level)
-
-        def total(side_of, m):
-            value = part[level, side_of, y, m].astype(F32)
+        n = span(level)
+        arrived(got.at[level, :, :, pl.ds(0, n)], S_RY + level)
+
+        def total(side_of, half, first, m):
+            value = part[level, side_of, y, first + m].astype(F32)
             for i in range(2):
-                value = value + got[level, side_of, i, m].astype(F32)
+                value = value + got[level, half, i, m].astype(F32)
             return value
 
+        if level in ACROSS_FIRST:
+
+            def both(m):
+                acc[level, m] = total(xl, 0, 0, m)
+                acc[level, 4 + m] = total(xl, 1, 4, m)
+
+            loop(4, both, 4)
+            return
+
         def give(m):
-            mid[level, m] = total(1 - xl, m).astype(BF)
+            mid[level, m] = total(1 - xl, 1 - xl, 0, m).astype(BF)
 
         def keep(m):
-            acc[level, m] = total(xl, m)
+            acc[level, m] = total(xl, xl, 0, m)
 
         loop(8, give, 4)
         send(mid.at[level], other.at[level], S_RX + level, across)
         loop(8, keep, 4)
 
     def finish(level, out, at):
-        arrived(other.at[level], S_RX + level)
-
-        def body(m):
-            acc[level, m] = acc[level, m] + other[level, m].astype(F32)
-
-        loop(8, body, 4)
+        if level not in ACROSS_FIRST:
+            arrived(other.at[level], S_RX + level)
+
+            def body(m):
+                acc[level, m] = acc[level, m] + other[level, m].astype(F32)
+
+            loop(8, body, 4)
         for u in range(2):
             first = 8 * c + 4 * u if level % 4 < 3 else 8 * u + 4 * c
             dst = out.at[at, pl.ds(first, 4)]
@@ -271,72 +326,69 @@
         backward(gt, lv, 2**lv, weights_high(lv))
     to_tensor(lambda j: gt.at[0, j], go.at[4, t], S_GA)
 
+    def forth(level):
+        forward(xt, level - 4, 2 ** (level - 4), weights_high(level - 4))
+
+    def back(level):
+        backward(go, level, 2**level, weights_low(level))
+
+    def end(level):
+        finish(level, *((fgrad, level) if level < 4 else (fin, level - 4)))
+
+    def mix_out(_):
+        own = pl.ds(pl.multiple_of(t * 128, 128), 128)
+        to_tensor(lambda j: xt.at[4, j], mixed.at[:, own], S_MA)
+
+    def grad_home(_):
+        arrived(go.at[4], S_GA)
+
+    def token_out(_):
+        loop(16, lambda j: local(go.at[0, j], tgrad.at[:, pl.ds(pl.multiple_of(j * 128, 128), 128)], S_TG))
+
+    def high_out(g):
+        for lv in (2 * g, 2 * g + 1):
+            arrived(fin.at[lv], S_FS + 4 + lv)
+
+        def pack(h):
+            for lv in (2 * g, 2 * g + 1):
+                hs[h, lv] = fin[lv, h].reshape(16, 128).astype(BF)
+
+        loop(16, pack, 4)
+        two = pl.ds(2 * g, 2)
+        to_tensor(lambda j: hs.at[j, two], hr.at[t, two], (S_HA, S_HB)[g])
+
+    def high_in(g):
+        two = pl.ds(2 * g, 2)
+        arrived(hr.at[:, two], (S_HA, S_HB)[g])
+
+        def unpack(j):
+            for lv in (2 * g, 2 * g + 1):
+                ob[lv, j] = hr[j, lv].astype(F32).reshape(2, 8, 128)
+
+        loop(16, unpack, 4)
+        local(ob.at[two], fgrad.at[pl.ds(4 + 2 * g, 2)], (S_OB, S_OC)[g])
+
+    steps = dict(
+        o=grad_out, i=grad_in, f=forth, b=back, r=relay, g=gather, m=meet, e=end,
+        M=mix_out, G=grad_home, T=token_out, H=high_out, I=high_in,
+    )
     arrived(xt.at[0], S_XA)
-    for level in range(4, 8):
-        grad_out(level)
-        forward(xt, level - 4, 2 ** (level - 4), weights_high(level - 4))
-        if level > 4:
-            grad_in(level - 1)
-        if level > 5:
-            relay(level - 2)
-    to_tensor(lambda j: xt.at[4, j], mixed.at[:, pl.ds(pl.multiple_of(t * 128, 128), 128)], S_MA)
-    grad_in(7)
-
-    relay(6)
-    gather(4)
-
-    arrived(go.at[4], S_GA)
-    for level in (3, 2, 1, 0):
-        grad_out(level)
-        backward(go, level, 2**level, weights_low(level))
-        grad_in(level)
-        relay(7 if level == 3 else level + 1)
-        if level > 0:
-            gather(8 - level)
-    loop(16, lambda j: local(go.at[0, j], tgrad.at[:, pl.ds(pl.multiple_of(j * 128, 128), 128)], S_TG))
-
-    for level in range(4, 8):
-        finish(level, fin, level - 4)
-    for level in range(4, 8):
-        arrived(fin.at[level - 4], S_FS + level)
-
-    def pack(h):
-        for lv in range(4):
-            hs[h, lv] = fin[lv, h].reshape(16, 128).astype(BF)
-
-    loop(16, pack)
-    to_tensor(lambda j: hs.at[j], hr.at[t], S_HA)
-
-    gather(3)
-    relay(0)
-    gather(2)
-    finish(3, fgrad, 3)
-    gather(1)
-    finish(2, fgrad, 2)
-    gather(0)
-    finish(1, fgrad, 1)
-    finish(0, fgrad, 0)
-
-    arrived(hr, S_HA)
-
-    def unpack(j):
-        for lv in range(4):
-            ob[lv, j] = hr[j, lv].astype(F32).reshape(2, 8, 128)
-
-    loop(16, unpack)
-    local(ob, fgrad.at[pl.ds(4, 4)], S_OB)
+    for step in ORDER:
+        steps[step[0]](int(step[1]))
 
     for level in range(4):
         arrived(fgrad.at[level], S_FS + level)
     arrived(mixed, S_MA)
     arrived(tgrad, S_TG)
-    arrived(fgrad.at[pl.ds(4, 4)], S_OB)
+    arrived(fgrad.at[pl.ds(4, 2)], S_OB)
+    arrived(fgrad.at[pl.ds(6, 2)], S_OC)
     blocks = xo.at[0, pl.ds(0, 15)]
     for slot in (S_CA, S_XA, S_GA, S_MA):
         left(blocks, slot)
     left(hs.at[pl.ds(0, 15), 0], S_FZ)
     left(hs.at[pl.ds(0, 15), pl.ds(0, 3)], S_FY)
-    left(hs.at[pl.ds(0, 15)], S_HA)
+    left(hs.at[pl.ds(0, 15), pl.ds(0, 2)], S_HA)
+    left(hs.at[pl.ds(0, 15), pl.ds(0, 2)], S_HB)
     for lv in range(4):
         left(wt.at[lv, 0, 0, 0], S_AX + lv)
         left(wt.at[lv, 0, :, pl.ds(0, 2)], S_AY + lv)
@@ -344,9 +396,9 @@
         left(wt.at[lv, 0], S_CF + lv)
     for level in range(8):
         left(csend.at[level], S_CD + level)
-        left(rel.at[level], S_RR + level)
-        left(got.at[level], S_RY + level)
-        left(mid.at[level], S_RX + level)
+        left(rel.at[level, :, pl.ds(0, span(level))], S_RR + level)
+        left(got.at[level, :, :, pl.ds(0, span(level))], S_RY + level)
+        left(part.at[level, 0] if level in ACROSS_FIRST else mid.at[level], S_RX + level)
         left(acc.at[level, :, :, pl.ds(0, 8)], S_FS + level)
 
 
@@ -384,6 +436,7 @@
             pltpu.VMEM((4, 16, 2, 128, 128), BF),
             pltpu.VMEM((4, 2, 2, 4, 16, 16, 128), BF),
             grads, grads, grads, two, two, pltpu.VMEM((8, 2, 2, 8, 2, 16, 128), BF), slab, slab,
+            pltpu.VMEM((2, 4, 8, 2, 16, 128), BF),
             pltpu.VMEM((8, 8, 2, 16, 128), F32),
             pltpu.VMEM((4, 16, 2, 8, 128), F32),
             pltpu.VMEM((16, 4, 16, 128), BF),

time: 91.4 us -> 90.7 us (level)
  no operation moved by 1% of the time
where the time goes in v4:
time: 90.7 us; the launch traced here: 90.6 us
  Pallas kernels  89.9 us (99%)
    pallas_call x1, Pallas kernels, per_device(): pl.pallas_call(kernel, out_shape=shapes, in_specs=[hbm] * 3, out_specs=[h...  87.3 us
    pallas_call x1, Pallas kernels, per_device(): pl.pallas_call(hand_over, out_shape=shapes, in_specs=[hbm] * 3, out_specs...  2.59 us

profile of v4, /device:TPU:1, one launch (start us, length us, event | category | flops | bytes accessed | tf_op | source)
XLA Modules:
  0.0 90.6 jit_solution(11772088078713467545)
XLA Ops:
  0.6 87.3 %butterfly.1 = (bf16[128,2048]{1,0:T(8,128)(2,1)}, bf16[128,2048]{1,0:T(8,128)(2,1)}, f32[8,16,2,8,128]{4,3,2,1,0:T(8,128)}) custom-call(bf16[128,2048]{1,0:T(8,128)(2,1)} %tok.1, bf16[8,16,2,128,128]{4,3,2,1,0:T(8,128)(2,1)} %fac.1, bf16[128,2048]{1,0:T(8,128)(2,1)} %cot.1), custom_call_target="tpu_custom_call" | custom-call | flops 3221225472 | bytes 12582912 | tf_op jit(solution)/shard_map/butterfly/pallas_call | solution.py:429
  88.0 2.6 %hand_over.1 = (bf16[128,2048]{1,0:T(8,128)(2,1)}, bf16[128,2048]{1,0:T(8,128)(2,1)}, f32[8,16,2,8,128]{4,3,2,1,0:T(8,128)}) custom-call(bf16[128,2048]{1,0:T(8,128)(2,1)} %get-tuple-element.6.a, bf16[128,2048]{1,0:T(8,128)(2,1)} %get-tuple-element.7.b, f32[8,16,2,8,128]{4,3,2,1,0:T(8,128)} %get-tuple-element.8.c), custom_call_target="tpu_custom_call" | custom-call | tf_op jit(solution)/shard_map/hand_over/pallas_call | solution.py:454

commit v5 on v4

--- a/solution.py
+++ b/solution.py
@@ -17,7 +17,7 @@
     "o4", "f4", "o5", "f5", "i4", "o6", "f6", "i5", "r4", "o7", "f7", "i6", "r5", "M0",
     "i7", "r6", "g4", "G0", "o3", "b3", "i3", "r7", "g5", "o2", "b2", "i2", "r3", "g6",
     "e4", "e5", "o1", "b1", "i1", "r2", "g7", "H0", "o0", "b0", "i0", "e6", "e7", "r1",
-    "T0", "H1", "g3", "r0", "g2", "e3", "g1", "e2", "I0", "g0", "e1", "I1", "e0",
+    "H1", "g3", "r0", "T0", "g2", "e3", "g1", "e2", "I0", "g0", "e1", "I1", "e0",
 )
 
 

time: 90.7 us -> 90.7 us (level)
  no operation moved by 1% of the time
where the time goes in v5:
time: 90.7 us; the launch traced here: 90.6 us
  Pallas kernels  89.9 us (99%)
    pallas_call x1, Pallas kernels, per_device(): pl.pallas_call(kernel, out_shape=shapes, in_specs=[hbm] * 3, out_specs=[h...  87.3 us
    pallas_call x1, Pallas kernels, per_device(): pl.pallas_call(hand_over, out_shape=shapes, in_specs=[hbm] * 3, out_specs...  2.59 us

profile of v5, /device:TPU:1, one launch (start us, length us, event | category | flops | bytes accessed | tf_op | source)
XLA Modules:
  0.0 90.6 jit_solution(4782758194142469695)
XLA Ops:
  0.6 87.3 %butterfly.1 = (bf16[128,2048]{1,0:T(8,128)(2,1)}, bf16[128,2048]{1,0:T(8,128)(2,1)}, f32[8,16,2,8,128]{4,3,2,1,0:T(8,128)}) custom-call(bf16[128,2048]{1,0:T(8,128)(2,1)} %tok.1, bf16[8,16,2,128,128]{4,3,2,1,0:T(8,128)(2,1)} %fac.1, bf16[128,2048]{1,0:T(8,128)(2,1)} %cot.1), custom_call_target="tpu_custom_call" | custom-call | flops 3221225472 | bytes 12582912 | tf_op jit(solution)/shard_map/butterfly/pallas_call | solution.py:429
  88.0 2.6 %hand_over.1 = (bf16[128,2048]{1,0:T(8,128)(2,1)}, bf16[128,2048]{1,0:T(8,128)(2,1)}, f32[8,16,2,8,128]{4,3,2,1,0:T(8,128)}) custom-call(bf16[128,2048]{1,0:T(8,128)(2,1)} %get-tuple-element.6.a, bf16[128,2048]{1,0:T(8,128)(2,1)} %get-tuple-element.7.b, f32[8,16,2,8,128]{4,3,2,1,0:T(8,128)} %get-tuple-element.8.c), custom_call_target="tpu_custom_call" | custom-call | tf_op jit(solution)/shard_map/hand_over/pallas_call | solution.py:454
